TPU v7x, 32 devices: a whole 2x2x4 slice. The times are simulated.
32 devices in a mesh: radial: 8 (over y, x, core), axial: 4 (over z).
Axes of the slice: x: 2, y: 2, z: 4, core: 2. Of those that a mesh axis runs over, the one named last changes fastest.
Arguments:
- rhs: float32 [2, 2, 96, 64, 512], P(None, None, None, 'radial', 'axial'), may hold values from -6 to 6
- mat_ids: int32 [96, 64, 512], P(None, 'radial', 'axial'), may hold values from 0 to 3
- stiff_table: float32 [4], replicated, may hold values from 0.5 to 4
- dens_table: float32 [4], replicated, may hold values from 0.5 to 2
- mass_shift: float32 [2], replicated, may hold values from 0.5 to 2
- harmonic: int32 [2], replicated, may hold values from 1 to 12
- radial_factor: float32 [2, 2, 16, 16], replicated, may hold values from -0.09375 to 0.09375
- axial_factor: float32 [2, 2, 64, 64], replicated, may hold values from -0.046875 to 0.046875
Outputs:
- solution: float32 [2, 2, 96, 64, 512], P(None, None, None, 'radial', 'axial')
- residual: float32 [2, 2, 96, 64, 512], P(None, None, None, 'radial', 'axial')
All inputs are finite; a program needn't handle non-finite values.
Results may differ from a plain program's by a relative error of at most 0.00021.
Values sent between devices are 32-bit elements; how exact they have to be, the bound alone decides.
A program may use at most 128 MiB of HBM per device.

v0:
```python
import jax
import jax.numpy as jnp
from jax import lax
from jax.sharding import PartitionSpec as P

ITERS = 3
NSECT = 24
AR = 4
AA = 8


LOSS_FACTOR = 0.2
RELAXATION = 0.6


def extended(shard, sides, width):
    for axis, dim in sides:
        size, length = (lax.axis_size(axis), shard.shape[dim])
        up = [(i, (i + 1) % size) for i in range(size - 1)]
        down = [(j, i) for i, j in up]
        last = lax.slice_in_dim(shard, length - width, length, axis=dim)
        first = lax.slice_in_dim(shard, 0, width, axis=dim)
        before = lax.ppermute(last, axis, up)
        after = lax.ppermute(first, axis, down)
        shard = jnp.concatenate([before, shard, after], axis=dim)
    return shard


def material(mat_ids, table):
    result = jnp.zeros(mat_ids.shape, table.dtype)
    for entry in range(table.shape[0]):
        result = result + jnp.where(mat_ids == entry, table[entry], jnp.zeros((), table.dtype))
    return result


def couplings(stiffness, padded):
    return (
        0.5 * (stiffness + padded[:, 2:, 1:-1]),
        0.5 * (stiffness + padded[:, :-2, 1:-1]),
        0.5 * (stiffness + padded[:, 1:-1, 2:]),
        0.5 * (stiffness + padded[:, 1:-1, :-2]),
        0.5 * (stiffness + jnp.roll(stiffness, -1, 0)),
        0.5 * (stiffness + jnp.roll(stiffness, 1, 0)),
    )


def neighbours(values, padded, weights, cosines, sines):
    summed = weights[0] * padded[:, :, :, 2:, 1:-1] + weights[1] * padded[:, :, :, :-2, 1:-1]
    summed = (
        summed + weights[2] * padded[:, :, :, 1:-1, 2:] + weights[3] * padded[:, :, :, 1:-1, :-2]
    )
    real_part = values[0]
    imag_part = values[1]
    cosine = cosines[:, None, None, None]
    sine = sines[:, None, None, None]
    wrap_real = cosine * real_part[:, :1] - sine * imag_part[:, :1]
    wrap_imag = sine * real_part[:, :1] + cosine * imag_part[:, :1]
    ahead = jnp.stack(
        [
            jnp.concatenate([real_part[:, 1:], wrap_real], 1),
            jnp.concatenate([imag_part[:, 1:], wrap_imag], 1),
        ]
    )
    back_real = cosine * real_part[:, -1:] + sine * imag_part[:, -1:]
    back_imag = cosine * imag_part[:, -1:] - sine * real_part[:, -1:]
    behind = jnp.stack(
        [
            jnp.concatenate([back_real, real_part[:, :-1]], 1),
            jnp.concatenate([back_imag, imag_part[:, :-1]], 1),
        ]
    )
    return summed + weights[4] * ahead + weights[5] * behind


def operate(values, weights, diag_real, diag_imag, cosines, sines):
    padded = extended(values, (("radial", 3), ("axial", 4)), 1)
    coupled = neighbours(values, padded, weights, cosines, sines)
    real_out = (
        diag_real * values[0] - diag_imag * values[1] - (coupled[0] - LOSS_FACTOR * coupled[1])
    )
    imag_out = (
        diag_real * values[1] + diag_imag * values[0] - (coupled[1] + LOSS_FACTOR * coupled[0])
    )
    return jnp.stack([real_out, imag_out])


def right_product(left_real, left_imag, right_real, right_imag):

    def matmul(first, second):
        return jnp.einsum("hij,hkj->hik", first, second, precision=lax.Precision.HIGHEST)

    return (
        matmul(left_real, right_real) - matmul(left_imag, right_imag),
        matmul(left_real, right_imag) + matmul(left_imag, right_real),
    )


def left_product(left_real, left_imag, right_real, right_imag):

    def matmul(first, second):
        return jnp.einsum("hij,hjk->hik", first, second, precision=lax.Precision.HIGHEST)

    return (
        matmul(left_real, right_real) - matmul(left_imag, right_imag),
        matmul(left_real, right_imag) + matmul(left_imag, right_real),
    )


def jacobi_step(residual, diag_real, diag_imag):
    scale = RELAXATION / (diag_real * diag_real + diag_imag * diag_imag)
    real_out = (diag_real * residual[0] + diag_imag * residual[1]) * scale
    imag_out = (diag_real * residual[1] - diag_imag * residual[0]) * scale
    return jnp.stack([real_out, imag_out])


def coarse_correction(residual, radial_factor, axial_factor):
    shape = residual.shape
    band_rows = shape[3] // AR
    band_cols = shape[4] // AA
    blocks = residual.reshape(2, shape[1], shape[2], band_rows, AR, band_cols, AA)
    coarse_res = jnp.sum(blocks, axis=(2, 4, 6))
    mine_axial = lax.dynamic_slice_in_dim(
        axial_factor, lax.axis_index("axial") * band_cols, band_cols, 2
    )
    mine_radial = lax.dynamic_slice_in_dim(
        radial_factor, lax.axis_index("radial") * band_rows, band_rows, 2
    )
    radial_count = lax.axis_size("radial")
    axial_count = lax.axis_size("axial")
    collected = lax.all_gather(coarse_res[None], ("radial", "axial"), axis=0, tiled=True)
    collected = collected.reshape(radial_count, axial_count, 2, shape[1], band_rows, band_cols)
    collected = collected.transpose(2, 3, 0, 4, 1, 5).reshape(
        2, shape[1], radial_count * band_rows, axial_count * band_cols
    )
    mixed_real, mixed_imag = right_product(collected[0], collected[1], mine_axial[0], mine_axial[1])
    corr_real, corr_imag = left_product(mine_radial[0], mine_radial[1], mixed_real, mixed_imag)
    spread = jnp.repeat(jnp.repeat(jnp.stack([corr_real, corr_imag]), AR, axis=2), AA, axis=3)
    return spread[:, :, None]


def local(rhs, mat_ids, stiff_table, dens_table, mass_shift, harmonic, radial_factor, axial_factor):
    stiffness = material(mat_ids, stiff_table)
    density = material(mat_ids, dens_table)
    padded_stiff = extended(stiffness, (("radial", 1), ("axial", 2)), 1)
    weights = couplings(stiffness, padded_stiff)
    total = weights[0] + weights[1] + weights[2] + weights[3] + weights[4] + weights[5]
    diag_real = total[None] - mass_shift[:, None, None, None] * density[None]
    diag_imag = LOSS_FACTOR * total
    angles = 2.0 * jnp.pi / NSECT * harmonic.astype(jnp.float32)
    cosines = jnp.cos(angles)
    sines = jnp.sin(angles)
    solution = jnp.zeros_like(rhs)
    residual = rhs
    for iteration in range(ITERS):
        if iteration > 0:
            residual = rhs - operate(solution, weights, diag_real, diag_imag, cosines, sines)
        correction = coarse_correction(residual, radial_factor, axial_factor)
        solution = solution + jacobi_step(residual, diag_real, diag_imag) + correction
    residual = rhs - operate(solution, weights, diag_real, diag_imag, cosines, sines)
    return (solution, residual)


def solution(mesh):
    return jax.shard_map(
        local,
        mesh=mesh,
        in_specs=(
            P(None, None, None, "radial", "axial"),
            P(None, "radial", "axial"),
            P(),
            P(),
            P(),
            P(),
            P(),
            P(),
        ),
        out_specs=(P(None, None, None, "radial", "axial"), P(None, None, None, "radial", "axial")),
        check_vma=False,
    )
```

profile of v0, /device:TPU:12, one launch (start us, length us, event | category | flops | bytes accessed | tf_op | source)
XLA Modules:
  0.0 395.2 jit_solution(4183586601979156998)
XLA Ops:
  3.6 4.6 %select_add_fusion = (f32[96,8,128]{2,0,1:T(8,128)}, pred[96,8,128]{2,0,1:T(8,128)(4,1)S(1)}, pred[96,8,128]{2,0,1:T(8,128)(4,1)S(1)}, pred[96,8,128]{2,0,1:T(8,128)(4,1)S(1)}, pred[96,8,128]{2,0,1:T(8,128)(4,1)S(1)}) fusion(f32[]{:T(128)} %bitcast.7, f32[]{:T(128)} %bitcast.6, f32[]{:T(128)} %bitcast.5, f32[]{:T(128)} %bitcast.4, s32[96,8,128]{2,1,0:T(8,128)} %param.9), kind=kLoop, calls=%fused_computation.139 | loop fusion | flops 1081344 | bytes 1179664 | tf_op jit(solution)/shard_map/add | solution.py:32
  8.2 2.8 select_add_fusion.1
  13.0 4.5 %collective-permute-start = (f32[96,1,128]{2,0,1:T(8,128)S(1)}, f32[96,1,128]{2,0,1:T(8,128)S(1)}, u32[]{:S(2)}, u32[]{:S(2)}) collective-permute-start(f32[96,1,128]{2,0,1:T(8,128)S(1)} %get-tuple-element.85), channel_id=1, source_target_pairs={{4,0},{8,4},{12,8},{16,12},{20,16},{24,20},{28,24},{5,1},{9,5},{13... | collective-permute-start | bytes 147464 | tf_op jit(solution)/shard_map/ppermute | solution.py:24
  18.9 65.0 %all-gather = f32[64,2,2,16]{3,2,1,0:T(2,128)S(1)} all-gather(f32[2,2,2,16]{3,2,1,0:T(2,128)S(1)} %reduce_sum.38), channel_id=2, replica_groups=mesh['radial'=8,'axial'=4] {'radial','axial'}, dimensions={0}, use_global_device_ids=true | all-gather | bytes 16896 | tf_op jit(solution)/shard_map/all_gather | solution.py:130
  89.5 4.8 %collective-permute-start.2 = (f32[96,10,1]{0,1,2:T(8,128)S(1)}, f32[96,10,1]{0,1,2:T(8,128)S(1)}, u32[]{:S(2)}, u32[]{:S(2)}) collective-permute-start(f32[96,10,1]{0,1,2:T(8,128)S(1)} %copy.253), channel_id=1, source_target_pairs={{1,0},{2,1},{3,2},{5,4},{6,5},{7,6},{9,8},{10,9},{11,10},{13,12},{... | collective-permute-start | bytes 11528 | tf_op jit(solution)/shard_map/ppermute | solution.py:24
  101.1 2.9 broadcast_multiply_fusion
  109.0 2.4 collective-permute-start.5
  118.1 3.6 fusion.83
  126.0 3.0 copy.222
  129.0 4.2 %collective-permute-start.6 = (f32[2,2,96,10,1]{2,1,4,3,0:T(2,128)}, f32[2,2,96,10,1]{2,1,4,3,0:T(2,128)}, u32[]{:S(2)}, u32[]{:S(2)}) collective-permute-start(f32[2,2,96,10,1]{2,1,4,3,0:T(2,128)} %copy.222), channel_id=1, source_target_pairs={{1,0},{2,1},{3,2},{5,4},{6,5},{7,6},{9,8},{10,9},{11,10},{13,12},{... | collective-permute-start | bytes 46088 | tf_op jit(solution)/shard_map/ppermute | solution.py:24
  143.6 3.1 copy.223
  146.7 6.0 %fusion.21 = f32[2,2,96,8,128]{4,3,2,1,0:T(8,128)S(1)} fusion(f32[2,2,96,10,1]{4,3,2,1,0:T(8,128)} %copy.226, f32[2,2,96,1,128]{4,3,2,1,0:T(1,128)S(1)} %collective-permute-done.4, f32[2,2,96,8,128]{4,3,2,1,0:T(8,128)S(1)} %maximum_add_fusion, f32[2,2,96,1,128]{4,3,2,1,0:T(1,128)} %copy-done.32, f32[2,2,96,10,1]{4,3,2,1,0:T(8,128)} %copy.223, ...), kind=kLoop, calls=%fused_computation.41 | loop fusion | flops 8257536 | bytes 9074688 | tf_op jit(solution)/shard_map/add | solution.py:72
  157.4 64.0 %all-gather.1 = f32[64,2,2,16]{3,2,1,0:T(2,128)S(1)} all-gather(f32[2,2,2,16]{3,2,1,0:T(2,128)S(1)} %copy.250), channel_id=3, replica_groups=mesh['radial'=8,'axial'=4] {'radial','axial'}, dimensions={0}, use_global_device_ids=true | all-gather | bytes 16896 | tf_op jit(solution)/shard_map/all_gather | solution.py:130
  221.9 3.0 add_multiply_fusion.1
  234.5 2.4 collective-permute-start.9
  239.7 2.7 collective-permute-done.9
  243.6 3.6 fusion.82
  251.5 3.0 copy.234
  254.5 4.1 %collective-permute-start.10 = (f32[2,2,96,10,1]{2,1,4,3,0:T(2,128)}, f32[2,2,96,10,1]{2,1,4,3,0:T(2,128)}, u32[]{:S(2)}, u32[]{:S(2)}) collective-permute-start(f32[2,2,96,10,1]{2,1,4,3,0:T(2,128)} %copy.234), channel_id=1, source_target_pairs={{1,0},{2,1},{3,2},{5,4},{6,5},{7,6},{9,8},{10,9},{11,10},{13,12},{... | collective-permute-start | bytes 46088 | tf_op jit(solution)/shard_map/ppermute | solution.py:24
  263.1 3.1 copy.235
  266.2 6.0 %fusion.12 = f32[2,2,96,8,128]{4,3,2,1,0:T(8,128)S(1)} fusion(f32[2,2,96,10,1]{4,3,2,1,0:T(8,128)} %copy.237, f32[2,2,96,1,128]{4,3,2,1,0:T(1,128)S(1)} %collective-permute-done.8, f32[2,2,96,8,128]{4,3,2,1,0:T(8,128)S(1)} %fusion.27, f32[2,2,96,1,128]{4,3,2,1,0:T(1,128)} %copy-done.34, f32[2,2,96,10,1]{4,3,2,1,0:T(8,128)} %copy.235, ...), kind=kLoop, calls=%fused_computation.24 | loop fusion | flops 8257536 | bytes 9074688 | tf_op jit(solution)/shard_map/add | solution.py:72
  276.9 64.0 %all-gather.2 = f32[64,2,2,16]{3,2,1,0:T(2,128)S(1)} all-gather(f32[2,2,2,16]{3,2,1,0:T(2,128)S(1)} %copy.252), channel_id=4, replica_groups=mesh['radial'=8,'axial'=4] {'radial','axial'}, dimensions={0}, use_global_device_ids=true | all-gather | bytes 16896 | tf_op jit(solution)/shard_map/all_gather | solution.py:130
  341.4 3.0 add_multiply_fusion
  348.5 2.6 fusion.28
  355.1 2.4 collective-permute-start.13
  360.4 2.6 collective-permute-done.13
  364.3 3.6 fusion.81
  367.9 2.6 copy.245
  372.4 3.2 copy.243
  375.6 4.2 %collective-permute-start.14 = (f32[2,2,96,10,1]{2,3,4,1,0:T(8,128)}, f32[2,2,96,10,1]{2,3,4,1,0:T(8,128)}, u32[]{:S(2)}, u32[]{:S(2)}) collective-permute-start(f32[2,2,96,10,1]{2,3,4,1,0:T(8,128)} %copy.243), channel_id=1, source_target_pairs={{1,0},{2,1},{3,2},{5,4},{6,5},{7,6},{9,8},{10,9},{11,10},{13,12},{... | collective-permute-start | bytes 46088 | tf_op jit(solution)/shard_map/ppermute | solution.py:24
  384.2 3.1 copy.244
  387.3 6.0 %fusion.3 = f32[2,2,96,8,128]{4,3,2,1,0:T(8,128)S(1)} fusion(f32[2,2,96,10,1]{4,3,2,1,0:T(8,128)} %copy.246, f32[2,2,96,1,128]{4,3,2,1,0:T(1,128)S(1)} %collective-permute-done.12, f32[2,2,96,8,128]{4,3,2,1,0:T(8,128)S(1)} %fusion.28, f32[2,2,96,1,128]{4,3,2,1,0:T(1,128)} %copy-done.33, f32[2,2,96,10,1]{4,3,2,1,0:T(8,128)} %copy.244, ...), kind=kLoop, calls=%fused_computation.7 | loop fusion | flops 8257536 | bytes 9074688 | tf_op jit(solution)/shard_map/add | solution.py:72
  (237 shorter events, 97.8 us)
Async XLA Ops:
  0.6 83.5 %copy-start = (f32[2,2,64,64]{3,2,1,0:T(8,128)S(1)}, f32[2,2,64,64]{3,2,1,0:T(8,128)}, u32[]{:S(2)}) copy-start(f32[2,2,64,64]{3,2,1,0:T(8,128)} %param.15) | copy-start | bytes 196612
  8.2 10.3 %copy-start.2 = (f32[2,2,96,8,128]{4,3,2,1,0:T(8,128)S(1)}, f32[2,2,96,8,128]{4,3,2,1,0:T(8,128)}, u32[]{:S(2)}) copy-start(f32[2,2,96,8,128]{4,3,2,1,0:T(8,128)} %param.8) | copy-start | bytes 4718596
  11.1 77.8 %collective-permute-start.1 = (f32[96,1,128]{2,0,1:T(8,128)S(1)}, f32[96,1,128]{2,0,1:T(8,128)S(1)}, u32[]{:S(2)}, u32[]{:S(2)}) collective-permute-start(f32[96,1,128]{2,0,1:T(8,128)S(1)} %get-tuple-element.86), channel_id=1, source_target_pairs={{0,4},{4,8},{8,12},{12,16},{16,20},{20,24},{24,28},{1,5},{5,9},{9,... | collective-permute-start | bytes 147464 | tf_op jit(solution)/shard_map/ppermute | solution.py:23
  13.0 75.9 %collective-permute-start = (f32[96,1,128]{2,0,1:T(8,128)S(1)}, f32[96,1,128]{2,0,1:T(8,128)S(1)}, u32[]{:S(2)}, u32[]{:S(2)}) collective-permute-start(f32[96,1,128]{2,0,1:T(8,128)S(1)} %get-tuple-element.85), channel_id=1, source_target_pairs={{4,0},{8,4},{12,8},{16,12},{20,16},{24,20},{28,24},{5,1},{9,5},{13... | collective-permute-start | bytes 147464 | tf_op jit(solution)/shard_map/ppermute | solution.py:24
  18.5 68.9 %copy-start.42 = (s32[2]{0:T(128)S(1)}, s32[2]{0:T(128)}, u32[]{:S(2)}) copy-start(s32[2]{0:T(128)} %param.13) | copy-start | bytes 28
  89.5 8.5 %collective-permute-start.2 = (f32[96,10,1]{0,1,2:T(8,128)S(1)}, f32[96,10,1]{0,1,2:T(8,128)S(1)}, u32[]{:S(2)}, u32[]{:S(2)}) collective-permute-start(f32[96,10,1]{0,1,2:T(8,128)S(1)} %copy.253), channel_id=1, source_target_pairs={{1,0},{2,1},{3,2},{5,4},{6,5},{7,6},{9,8},{10,9},{11,10},{13,12},{... | collective-permute-start | bytes 11528 | tf_op jit(solution)/shard_map/ppermute | solution.py:24
  94.5 5.7 %collective-permute-start.3 = (f32[96,10,1]{0,1,2:T(8,128)S(1)}, f32[96,10,1]{0,1,2:T(8,128)}, u32[]{:S(2)}, u32[]{:S(2)}) collective-permute-start(f32[96,10,1]{0,1,2:T(8,128)S(1)} %copy.254), channel_id=1, source_target_pairs={{0,1},{1,2},{2,3},{4,5},{5,6},{6,7},{8,9},{9,10},{10,11},{12,13},{... | collective-permute-start | bytes 11528 | tf_op jit(solution)/shard_map/ppermute | solution.py:23
  97.7 7.0 %copy-start.3 = (f32[96,8,128]{2,1,0:T(8,128)}, f32[96,8,128]{2,1,0:T(8,128)S(1)}, u32[]{:S(2)}) copy-start(f32[96,8,128]{2,1,0:T(8,128)S(1)} %copy.213) | copy-start | bytes 1179652
  107.0 8.4 %collective-permute-start.4 = (f32[2,2,96,1,128]{4,3,2,1,0:T(1,128)S(1)}, f32[2,2,96,1,128]{4,3,2,1,0:T(1,128)S(1)}, u32[]{:S(2)}, u32[]{:S(2)}) collective-permute-start(f32[2,2,96,1,128]{4,3,2,1,0:T(1,128)S(1)} %get-tuple-element.66), channel_id=1, source_target_pairs={{4,0},{8,4},{12,8},{16,12},{20,16},{24,20},{28,24},{5,1},{9,5},{13... | collective-permute-start | bytes 589832 | tf_op jit(solution)/shard_map/ppermute | solution.py:24
  109.0 7.9 %collective-permute-start.5 = (f32[2,2,96,1,128]{4,3,2,1,0:T(1,128)S(1)}, f32[2,2,96,1,128]{4,3,2,1,0:T(1,128)S(1)}, u32[]{:S(2)}, u32[]{:S(2)}) collective-permute-start(f32[2,2,96,1,128]{4,3,2,1,0:T(1,128)S(1)} %get-tuple-element.65), channel_id=1, source_target_pairs={{0,4},{4,8},{8,12},{12,16},{16,20},{20,24},{24,28},{1,5},{5,9},{9,... | collective-permute-start | bytes 589832 | tf_op jit(solution)/shard_map/ppermute | solution.py:23
  124.1 17.2 %collective-permute-start.7 = (f32[2,2,96,10,1]{2,1,4,3,0:T(2,128)S(1)}, f32[2,2,96,10,1]{2,1,4,3,0:T(2,128)S(1)}, u32[]{:S(2)}, u32[]{:S(2)}) collective-permute-start(f32[2,2,96,10,1]{2,1,4,3,0:T(2,128)S(1)} %copy.225), channel_id=1, source_target_pairs={{0,1},{1,2},{2,3},{4,5},{5,6},{6,7},{8,9},{9,10},{10,11},{12,13},{... | collective-permute-start | bytes 46088 | tf_op jit(solution)/shard_map/ppermute | solution.py:23
  129.0 6.4 %copy-start.31 = (f32[96,8,128]{2,0,1:T(8,128)S(1)}, f32[96,8,128]{2,0,1:T(8,128)}, u32[]{:S(2)}) copy-start(f32[96,8,128]{2,0,1:T(8,128)} %get-tuple-element.24) | copy-start | bytes 1179652
  129.0 7.3 %copy-start.30 = (f32[96,8,128]{2,0,1:T(8,128)S(1)}, f32[96,8,128]{2,0,1:T(8,128)}, u32[]{:S(2)}) copy-start(f32[96,8,128]{2,0,1:T(8,128)} %get-tuple-element.23) | copy-start | bytes 1179652
  129.0 14.7 %collective-permute-start.6 = (f32[2,2,96,10,1]{2,1,4,3,0:T(2,128)}, f32[2,2,96,10,1]{2,1,4,3,0:T(2,128)}, u32[]{:S(2)}, u32[]{:S(2)}) collective-permute-start(f32[2,2,96,10,1]{2,1,4,3,0:T(2,128)} %copy.222), channel_id=1, source_target_pairs={{1,0},{2,1},{3,2},{5,4},{6,5},{7,6},{9,8},{10,9},{11,10},{13,12},{... | collective-permute-start | bytes 46088 | tf_op jit(solution)/shard_map/ppermute | solution.py:24
  154.6 67.3 %copy-start.5 = (f32[96,8,128]{2,1,0:T(8,128)S(1)}, f32[96,8,128]{2,1,0:T(8,128)}, u32[]{:S(2)}) copy-start(f32[96,8,128]{2,1,0:T(8,128)} %copy-done.3) | copy-start | bytes 1179652
  154.6 67.3 %copy-start.11 = (f32[96,8,128]{2,1,0:T(8,128)S(1)}, f32[96,8,128]{2,1,0:T(8,128)}, u32[]{:S(2)}) copy-start(f32[96,8,128]{2,1,0:T(8,128)} %copy-done.9) | copy-start | bytes 1179652
  154.6 67.3 %copy-start.17 = (f32[96,8,128]{2,1,0:T(8,128)S(1)}, f32[96,8,128]{2,1,0:T(8,128)}, u32[]{:S(2)}) copy-start(f32[96,8,128]{2,1,0:T(8,128)} %copy-done.15) | copy-start | bytes 1179652
  154.6 67.4 %copy-start.24 = (f32[96,8,128]{2,1,0:T(8,128)S(1)}, f32[96,8,128]{2,1,0:T(8,128)}, u32[]{:S(2)}) copy-start(f32[96,8,128]{2,1,0:T(8,128)} %copy-done.23) | copy-start | bytes 1179652
  232.6 7.1 %collective-permute-start.8 = (f32[2,2,96,1,128]{4,3,2,1,0:T(1,128)S(1)}, f32[2,2,96,1,128]{4,3,2,1,0:T(1,128)S(1)}, u32[]{:S(2)}, u32[]{:S(2)}) collective-permute-start(f32[2,2,96,1,128]{4,3,2,1,0:T(1,128)S(1)} %get-tuple-element.62), channel_id=1, source_target_pairs={{4,0},{8,4},{12,8},{16,12},{20,16},{24,20},{28,24},{5,1},{9,5},{13... | collective-permute-start | bytes 589832 | tf_op jit(solution)/shard_map/ppermute | solution.py:24
  234.5 7.9 %collective-permute-start.9 = (f32[2,2,96,1,128]{4,3,2,1,0:T(1,128)S(1)}, f32[2,2,96,1,128]{4,3,2,1,0:T(1,128)S(1)}, u32[]{:S(2)}, u32[]{:S(2)}) collective-permute-start(f32[2,2,96,1,128]{4,3,2,1,0:T(1,128)S(1)} %get-tuple-element.61), channel_id=1, source_target_pairs={{0,4},{4,8},{8,12},{12,16},{16,20},{20,24},{24,28},{1,5},{5,9},{9,... | collective-permute-start | bytes 589832 | tf_op jit(solution)/shard_map/ppermute | solution.py:23
  249.6 11.1 %collective-permute-start.11 = (f32[2,2,96,10,1]{2,1,4,3,0:T(2,128)S(1)}, f32[2,2,96,10,1]{2,1,4,3,0:T(2,128)S(1)}, u32[]{:S(2)}, u32[]{:S(2)}) collective-permute-start(f32[2,2,96,10,1]{2,1,4,3,0:T(2,128)S(1)} %copy.236), channel_id=1, source_target_pairs={{0,1},{1,2},{2,3},{4,5},{5,6},{6,7},{8,9},{9,10},{10,11},{12,13},{... | collective-permute-start | bytes 46088 | tf_op jit(solution)/shard_map/ppermute | solution.py:23
  254.5 8.6 %collective-permute-start.10 = (f32[2,2,96,10,1]{2,1,4,3,0:T(2,128)}, f32[2,2,96,10,1]{2,1,4,3,0:T(2,128)}, u32[]{:S(2)}, u32[]{:S(2)}) collective-permute-start(f32[2,2,96,10,1]{2,1,4,3,0:T(2,128)} %copy.234), channel_id=1, source_target_pairs={{1,0},{2,1},{3,2},{5,4},{6,5},{7,6},{9,8},{10,9},{11,10},{13,12},{... | collective-permute-start | bytes 46088 | tf_op jit(solution)/shard_map/ppermute | solution.py:24
  266.2 6.0 %copy-start.37 = (f32[2]{0:T(128)S(1)}, f32[2]{0:T(128)}, u32[]{:S(2)}) copy-start(f32[2]{0:T(128)} %param.12) | copy-start | bytes 28
  274.0 67.3 %copy-start.7 = (f32[96,8,128]{2,1,0:T(8,128)S(1)}, f32[96,8,128]{2,1,0:T(8,128)}, u32[]{:S(2)}) copy-start(f32[96,8,128]{2,1,0:T(8,128)} %copy-done.3) | copy-start | bytes 1179652
  274.0 67.3 %copy-start.13 = (f32[96,8,128]{2,1,0:T(8,128)S(1)}, f32[96,8,128]{2,1,0:T(8,128)}, u32[]{:S(2)}) copy-start(f32[96,8,128]{2,1,0:T(8,128)} %copy-done.9) | copy-start | bytes 1179652
  274.0 67.3 %copy-start.19 = (f32[96,8,128]{2,1,0:T(8,128)S(1)}, f32[96,8,128]{2,1,0:T(8,128)}, u32[]{:S(2)}) copy-start(f32[96,8,128]{2,1,0:T(8,128)} %copy-done.15) | copy-start | bytes 1179652
  274.0 67.4 %copy-start.25 = (f32[96,8,128]{2,1,0:T(8,128)S(1)}, f32[96,8,128]{2,1,0:T(8,128)}, u32[]{:S(2)}) copy-start(f32[96,8,128]{2,1,0:T(8,128)} %copy-done.23) | copy-start | bytes 1179652
  351.1 42.2 %copy-start.1 = (f32[2,2,96,8,128]{4,3,2,1,0:T(8,128)}, f32[2,2,96,8,128]{4,3,2,1,0:T(8,128)S(1)}, u32[]{:S(2)}) copy-start(f32[2,2,96,8,128]{4,3,2,1,0:T(8,128)S(1)} %fusion.28) | copy-start | bytes 4718596
  353.2 7.2 %collective-permute-start.12 = (f32[2,2,96,1,128]{4,3,2,1,0:T(1,128)S(1)}, f32[2,2,96,1,128]{4,3,2,1,0:T(1,128)S(1)}, u32[]{:S(2)}, u32[]{:S(2)}) collective-permute-start(f32[2,2,96,1,128]{4,3,2,1,0:T(1,128)S(1)} %get-tuple-element.58), channel_id=1, source_target_pairs={{4,0},{8,4},{12,8},{16,12},{20,16},{24,20},{28,24},{5,1},{9,5},{13... | collective-permute-start | bytes 589832 | tf_op jit(solution)/shard_map/ppermute | solution.py:24
  355.1 7.9 %collective-permute-start.13 = (f32[2,2,96,1,128]{4,3,2,1,0:T(1,128)S(1)}, f32[2,2,96,1,128]{4,3,2,1,0:T(1,128)S(1)}, u32[]{:S(2)}, u32[]{:S(2)}) collective-permute-start(f32[2,2,96,1,128]{4,3,2,1,0:T(1,128)S(1)} %get-tuple-element.57), channel_id=1, source_target_pairs={{0,4},{4,8},{8,12},{12,16},{16,20},{20,24},{24,28},{1,5},{5,9},{9,... | collective-permute-start | bytes 589832 | tf_op jit(solution)/shard_map/ppermute | solution.py:23
  370.5 11.4 %collective-permute-start.15 = (f32[2,2,96,10,1]{2,3,4,1,0:T(8,128)S(1)}, f32[2,2,96,10,1]{2,3,4,1,0:T(8,128)S(1)}, u32[]{:S(2)}, u32[]{:S(2)}) collective-permute-start(f32[2,2,96,10,1]{2,3,4,1,0:T(8,128)S(1)} %copy.245), channel_id=1, source_target_pairs={{0,1},{1,2},{2,3},{4,5},{5,6},{6,7},{8,9},{9,10},{10,11},{12,13},{... | collective-permute-start | bytes 46088 | tf_op jit(solution)/shard_map/ppermute | solution.py:23
  375.6 8.7 %collective-permute-start.14 = (f32[2,2,96,10,1]{2,3,4,1,0:T(8,128)}, f32[2,2,96,10,1]{2,3,4,1,0:T(8,128)}, u32[]{:S(2)}, u32[]{:S(2)}) collective-permute-start(f32[2,2,96,10,1]{2,3,4,1,0:T(8,128)} %copy.243), channel_id=1, source_target_pairs={{1,0},{2,1},{3,2},{5,4},{6,5},{7,6},{9,8},{10,9},{11,10},{13,12},{... | collective-permute-start | bytes 46088 | tf_op jit(solution)/shard_map/ppermute | solution.py:24
  (27 other events, 80.8 us)
where the time goes:
time: 397 us; the launch traced here: 395 us
  blocking collectives  193 us (49%)
  local copies, waits for them, and re-layouts  70.6 us (18%)
  other arithmetic  65.2 us (16%)
  starting transfers between devices  44.3 us (11%)
  matrix products  11.9 us (3%)
  waiting for transfers between devices  8.7 us (2%)
    all_gather x3, blocking collectives, coarse_correction(): lax.all_gather(coarse_res[None], ('radial', 'axial'), axis=0, tiled=True)  193 us
    ppermute x8, starting transfers between devices, extended(): after = lax.ppermute(first, axis, down)  27.6 us
    slice x7, local copies, waits for them, and re-layouts, extended(): first = lax.slice_in_dim(shard, 0, width, axis=dim)  20 us
    add x3, other arithmetic, neighbours(): return summed + weights[4] * ahead + weights[5] * behind  18 us
    ppermute x8, starting transfers between devices, extended(): before = lax.ppermute(last, axis, up)  16.8 us
    dot_general x12, matrix products, matmul(): jnp.einsum('hij,hjk->hik', first, second, precision=lax.Precision.HIGHEST)  10.1 us
    ppermute x4, local copies, waits for them, and re-layouts, extended(): after = lax.ppermute(first, axis, down)  9.47 us
    another operation x6, other arithmetic, neighbours(): jnp.stack([jnp.concatenate([back_real, real_part[:, :-1]], 1), jnp.concat...  9.15 us
  transfers between devices with their start and end apart: 16, of which 4 were waited for; matrix products, arithmetic and copies ran while one was open for 12% of the time, Pallas kernels for 0%

commit v1 on v0

v1 whole, which is shorter than its diff:
```python
import functools

import jax
import jax.numpy as jnp
from jax import lax
from jax.experimental import pallas as pl
from jax.experimental.pallas import tpu as pltpu
from jax.sharding import PartitionSpec as P

ITERS = 3
NSECT = 24
AR = 4
AA = 8
LOSS_FACTOR = 0.2
RELAXATION = 0.6
MESH = pl.DeviceIdType.MESH
HIGHEST = lax.Precision.HIGHEST


def kernel(
    nrad,
    nax,
    rhs_ref,
    ids_ref,
    stiff_ref,
    dens_ref,
    mass_ref,
    harm_ref,
    radial_ref,
    axial_ref,
    sol_ref,
    res_ref,
    stiff,
    wr_up,
    wr_dn,
    wa_lo,
    wa_hi,
    wt,
    dr,
    di,
    sc,
    srow_s,
    srow_r,
    scol_s,
    scol_r,
    row_s,
    row_r,
    col_s,
    col_r,
    one_s,
    one_r,
    two_r,
    axmat,
    radmat,
    st_send,
    st_recv,
    ha_send,
    ha_recv,
    g1_send,
    g1_recv,
    g2_send,
    g2_recv,
):
    ct = rhs_ref.shape[2]
    rows, lanes = rhs_ref.shape[3:]
    gr = radial_ref.shape[2]
    ga = axial_ref.shape[2]
    band_r = rows // AR
    band_c = lanes // AA
    i = lax.axis_index("radial")
    j = lax.axis_index("axial")
    has_up, has_dn = i > 0, i < nrad - 1
    has_lo, has_hi = j > 0, j < nax - 1
    conds = (has_up, has_dn, has_lo, has_hi)
    targets = ({"radial": i - 1}, {"radial": i + 1}, {"axial": j - 1}, {"axial": j + 1})

    for d in range(4):

        @pl.when(jnp.logical_not(conds[d]))
        def _():
            if d < 2:
                srow_r[d] = jnp.zeros(srow_r.shape[1:], jnp.float32)
                for k in range(ITERS):
                    row_r[k, d] = jnp.zeros(row_r.shape[2:], jnp.float32)
            else:
                scol_r[d - 2] = jnp.zeros(scol_r.shape[1:], jnp.float32)
                for k in range(ITERS):
                    col_r[k, d - 2] = jnp.zeros(col_r.shape[2:], jnp.float32)

    barrier = pltpu.get_barrier_semaphore()
    for d in range(1, nax):
        pl.semaphore_signal(
            barrier, inc=1, device_id={"axial": lax.rem(j + d, nax)}, device_id_type=MESH
        )
    for d in range(1, nrad):
        pl.semaphore_signal(
            barrier, inc=1, device_id={"radial": lax.rem(i + d, nrad)}, device_id_type=MESH
        )

    row = lax.broadcasted_iota(jnp.int32, (rows, lanes), 0)
    lane = lax.broadcasted_iota(jnp.int32, (rows, lanes), 1)
    zero = jnp.zeros((rows, lanes), jnp.float32)

    def lookup(ids, table):
        value = jnp.full(ids.shape, table[0], jnp.float32)
        for entry in range(1, table.shape[0]):
            value = jnp.where(ids == entry, table[entry], value)
        return value

    def pack(value, t, first, last):
        first = jnp.where(lane == t, pltpu.roll(value, t, 1), first)
        last = jnp.where(lane == t, pltpu.roll(value, t + 1, 1), last)
        return first, last

    def stiff_copy(d):
        if d < 2:
            src, dst = srow_s.at[d], srow_r.at[1 - d]
        else:
            src, dst = scol_s.at[d - 2], scol_r.at[3 - d]
        return pltpu.make_async_remote_copy(
            src_ref=src,
            dst_ref=dst,
            send_sem=st_send.at[d],
            recv_sem=st_recv.at[d ^ 1],
            device_id=targets[d],
            device_id_type=MESH,
        )

    def halo_copy(k, d):
        if d < 2:
            src, dst = row_s.at[k, d], row_r.at[k, 1 - d]
        else:
            src, dst = col_s.at[k, d - 2], col_r.at[k, 3 - d]
        return pltpu.make_async_remote_copy(
            src_ref=src,
            dst_ref=dst,
            send_sem=ha_send.at[k, d],
            recv_sem=ha_recv.at[k, d ^ 1],
            device_id=targets[d],
            device_id_type=MESH,
        )

    def gather_one(k, d):
        return pltpu.make_async_remote_copy(
            src_ref=one_s.at[k],
            dst_ref=one_r.at[k, j],
            send_sem=g1_send.at[k, d],
            recv_sem=g1_recv.at[k, d],
            device_id={"axial": lax.rem(j + d, nax)},
            device_id_type=MESH,
        )

    def gather_two(k, d):
        return pltpu.make_async_remote_copy(
            src_ref=two_r.at[k, i],
            dst_ref=two_r.at[k, i],
            send_sem=g2_send.at[k, d],
            recv_sem=g2_recv.at[k, d],
            device_id={"radial": lax.rem(i + d, nrad)},
            device_id_type=MESH,
        )

    def on_faces(act):
        for d in range(4):

            @pl.when(conds[d])
            def _():
                act(d)

    def first_pass(t, carry):
        first, last, s0, s1, s2, s3 = carry
        value = lookup(ids_ref[t], stiff_ref)
        stiff[t + 1] = value
        srow_s[0, pl.ds(t, 1), :] = value[0:1]
        srow_s[1, pl.ds(t, 1), :] = value[rows - 1 : rows]
        first, last = pack(value, t, first, last)
        return (
            first,
            last,
            s0 + rhs_ref[0, 0, t],
            s1 + rhs_ref[0, 1, t],
            s2 + rhs_ref[1, 0, t],
            s3 + rhs_ref[1, 1, t],
        )

    first, last, *sums = lax.fori_loop(0, ct, first_pass, (zero,) * 6)
    scol_s[0] = first
    scol_s[1] = last
    stiff[0] = stiff[ct]
    stiff[ct + 1] = stiff[1]

    pl.semaphore_wait(barrier, nax + nrad - 2)
    on_faces(lambda d: stiff_copy(d).start())

    e_row = lax.broadcasted_iota(jnp.int32, (lanes, lanes), 0)
    e_col = lax.broadcasted_iota(jnp.int32, (lanes, lanes), 1)
    fold = jnp.where(e_row // AA + j * band_c == e_col, 1.0, 0.0)

    def restrict_and_send(k, sums):
        tile = zero
        for c in range(4):
            s = sums[c] + pltpu.roll(sums[c], rows - 1, 0)
            s = s + pltpu.roll(s, rows - 2, 0)
            for g in range(band_r):
                to = c * band_r + g
                moved = pltpu.roll(s, (to - g * AR) % rows, 0)
                tile = jnp.where(row == to, moved, tile)
        one_s[k] = jnp.dot(tile, fold, precision=HIGHEST, preferred_element_type=jnp.float32)
        for d in range(1, nax):
            gather_one(k, d).start()

    restrict_and_send(0, sums)

    ax_row = lax.broadcasted_iota(jnp.int32, (lanes, ga), 0)
    ax_col = lax.broadcasted_iota(jnp.int32, (lanes, ga), 1)
    own = jnp.where(ax_row // AA + j * band_c == ax_col, 1.0, 0.0)
    edge_lo = j * band_c - 1
    edge_hi = (j + 1) * band_c
    half = lanes // 2
    edges = []
    for p in range(2):
        hit = ((ax_row == p * half) & (ax_col == edge_lo)) | (
            (ax_row == p * half + 1) & (ax_col == edge_hi)
        )
        edges.append(jnp.where(hit, 1.0, 0.0))
    for h in range(2):
        if ga < lanes:
            axmat[h] = jnp.zeros(axmat.shape[1:], jnp.float32)

        def spread(select, p):
            return jnp.dot(
                select, axial_ref[p, h], precision=HIGHEST, preferred_element_type=jnp.float32
            )

        axmat[h, 0:lanes, 0:ga] = spread(own, 0)
        axmat[h, lanes : 2 * lanes, 0:ga] = spread(own, 1)
        axmat[h, 2 * lanes : 3 * lanes, 0:ga] = spread(edges[0], 0) + spread(edges[1], 1)

    per = 2 * rows
    cdev = 4 * band_r
    r_row = lax.broadcasted_iota(jnp.int32, (4 * per, gr), 0) % per
    r_col = lax.broadcasted_iota(jnp.int32, (4 * per, gr), 1)
    want = jnp.where(
        r_row < rows,
        r_row // AR + i * band_r,
        jnp.where(
            r_row == rows, i * band_r - 1, jnp.where(r_row == rows + 1, (i + 1) * band_r, -1)
        ),
    )
    r_sel = jnp.where(want == r_col, 1.0, 0.0)
    c_row = lax.broadcasted_iota(jnp.int32, (gr, nrad * cdev), 0)
    c_col = lax.broadcasted_iota(jnp.int32, (gr, nrad * cdev), 1)
    c_sel = jnp.where((c_col // cdev) * band_r + c_col % band_r == c_row, 1.0, 0.0)
    m_out = lax.broadcasted_iota(jnp.int32, (4 * per, nrad * cdev), 0) // per
    m_in = (lax.broadcasted_iota(jnp.int32, (4 * per, nrad * cdev), 1) % cdev) // band_r
    built = jnp.zeros((4 * per, nrad * cdev), jnp.float32)
    for h in range(2):
        for p in range(2):
            part = jnp.dot(
                jnp.dot(
                    r_sel, radial_ref[p, h], precision=HIGHEST, preferred_element_type=jnp.float32
                ),
                c_sel,
                precision=HIGHEST,
                preferred_element_type=jnp.float32,
            )
            if p == 0:
                built = jnp.where((m_out == m_in) & (m_out % 2 == h), part, built)
            else:
                built = jnp.where((m_out == h) & (m_in == 2 + h), -part, built)
                built = jnp.where((m_out == 2 + h) & (m_in == h), part, built)
    radmat[...] = built

    def mix_and_send(k):
        total = one_s[k]
        for d in range(1, nax):
            gather_one(k, d).wait_recv()
        for d in range(1, nax):
            total = total + one_r[k, lax.rem(j + d, nax)]
        outs = []
        for h in range(2):
            prod = lax.dot_general(
                total,
                axmat[h],
                (((1,), (1,)), ((), ())),
                precision=HIGHEST,
                preferred_element_type=jnp.float32,
            )
            a = prod[:, 0:lanes]
            b = prod[:, lanes : 2 * lanes]
            e = prod[:, 2 * lanes : 3 * lanes]
            f = pltpu.roll(e, half, 1)
            swap_b = pltpu.roll(b, rows // 2, 0)
            swap_f = pltpu.roll(f, rows // 2, 0)
            low = row < rows // 2
            outs.append(
                (jnp.where(low, a - swap_b, a + swap_b), jnp.where(low, e - swap_f, e + swap_f))
            )
        odd = (row // band_r) % 2 == 1
        two_r[k, i, :, 0:lanes] = jnp.where(odd, outs[1][0], outs[0][0])
        two_r[k, i, :, lanes : 2 * lanes] = jnp.where(odd, outs[1][1], outs[0][1])
        for d in range(1, nrad):
            gather_two(k, d).start()

    def finish_coarse(k):
        for d in range(1, nrad):
            gather_two(k, d).wait_recv()
        return jnp.dot(
            radmat[...],
            two_r[k].reshape(nrad * cdev, 2 * lanes),
            precision=HIGHEST,
            preferred_element_type=jnp.float32,
        )

    mix_and_send(0)
    on_faces(lambda d: stiff_copy(d ^ 1).wait_recv())

    mass = [mass_ref[0], mass_ref[1]]

    def around(value, up, dn, lo, hi, t):
        return (
            jnp.where(row == 0, up, pltpu.roll(value, 1, 0)),
            jnp.where(row == rows - 1, dn, pltpu.roll(value, rows - 1, 0)),
            jnp.where(lane == 0, pltpu.roll(lo, lax.rem(lanes - t, lanes), 1), pltpu.roll(value, 1, 1)),
            jnp.where(lane == lanes - 1, pltpu.roll(hi, lanes - 1 - t, 1), pltpu.roll(value, lanes - 1, 1)),
        )

    def put_halo(k, t, y, packs):
        out = []
        for c in range(4):
            row_s[k, 0, c, pl.ds(t, 1), :] = y[c][0:1]
            row_s[k, 1, c, pl.ds(t, 1), :] = y[c][rows - 1 : rows]
            out.extend(pack(y[c], t, packs[2 * c], packs[2 * c + 1]))
        return tuple(out)

    def smooth(t, rr, ri, h):
        d_re, d_im, scale = dr[h, t], di[t], sc[h, t]
        return (d_re * rr + d_im * ri) * scale, (d_re * ri - d_im * rr) * scale

    def setup_pass(t, packs):
        value = stiff[t + 1]
        up, dn, lo, hi = around(
            value,
            srow_r[0, pl.ds(t, 1), :],
            srow_r[1, pl.ds(t, 1), :],
            scol_r[0],
            scol_r[1],
            t,
        )
        c_up, c_dn = 0.5 * (value + up), 0.5 * (value + dn)
        c_lo, c_hi = 0.5 * (value + lo), 0.5 * (value + hi)
        c_be, c_ah = 0.5 * (value + stiff[t]), 0.5 * (value + stiff[t + 2])
        wr_up[t] = c_up
        wr_dn[t] = c_dn
        wa_lo[t] = c_lo
        wa_hi[t] = c_hi
        wt[t] = c_be
        wt[t + 1] = c_ah
        total = c_dn + c_up + c_hi + c_lo + c_ah + c_be
        density = lookup(ids_ref[t], dens_ref)
        d_im = LOSS_FACTOR * total
        di[t] = d_im
        y = [None] * 4
        for h in range(2):
            d_re = total - mass[h] * density
            scale = RELAXATION / (d_re * d_re + d_im * d_im)
            dr[h, t] = d_re
            sc[h, t] = scale
            rr, ri = rhs_ref[0, h, t], rhs_ref[1, h, t]
            y[h] = (d_re * rr + d_im * ri) * scale
            y[2 + h] = (d_re * ri - d_im * rr) * scale
            sol_ref[0, h, t] = y[h]
            sol_ref[1, h, t] = y[2 + h]
        return put_halo(0, t, y, packs)

    def send_halo(k, packs):
        for c in range(4):
            col_s[k, 0, c] = packs[2 * c]
            col_s[k, 1, c] = packs[2 * c + 1]
        on_faces(lambda d: halo_copy(k, d).start())

    send_halo(0, lax.fori_loop(0, ct, setup_pass, (zero,) * 8))

    cosines, sines = [], []
    for h in range(2):
        angle = jnp.full((rows, lanes), harm_ref[h], jnp.int32).astype(jnp.float32) * (
            2.0 * jnp.pi / NSECT
        )
        cosines.append(jnp.cos(angle))
        sines.append(jnp.sin(angle))

    for k in range(ITERS):
        final = k == ITERS - 1
        coarse = finish_coarse(k)
        corr = [coarse[c * per : c * per + rows, 0:lanes] for c in range(4)]
        on_faces(lambda d: halo_copy(k, d ^ 1).wait_recv())
        cols = []
        for c in range(4):
            for s in range(2):
                at = c * per + rows + s
                row_r[k, s, c] = row_r[k, s, c] + coarse[at : at + 1, 0:lanes]
                cols.append(
                    col_r[k, s, c]
                    + coarse[c * per : c * per + rows, lanes + s : lanes + s + 1]
                )
        for c in range(4):
            col_r[k, 0, c] = cols[2 * c]
            col_r[k, 1, c] = cols[2 * c + 1]

        def load(t):
            return [sol_ref[c // 2, c % 2, t] + corr[c] for c in range(4)]

        def turn(x, sign):
            return [cosines[h] * x[h] - sign * sines[h] * x[2 + h] for h in range(2)] + [
                sign * sines[h] * x[h] + cosines[h] * x[2 + h] for h in range(2)
            ]

        start = load(0)
        beyond = turn(start, 1.0)
        before = turn(load(ct - 1), -1.0)

        def stencil(t, xm, x, xp):
            c_up, c_dn, c_lo, c_hi = wr_up[t], wr_dn[t], wa_lo[t], wa_hi[t]
            c_be, c_ah = wt[t], wt[t + 1]
            nb = []
            for c in range(4):
                up, dn, lo, hi = around(
                    x[c],
                    row_r[k, 0, c, pl.ds(t, 1), :],
                    row_r[k, 1, c, pl.ds(t, 1), :],
                    col_r[k, 0, c],
                    col_r[k, 1, c],
                    t,
                )
                nb.append(
                    (c_dn * dn + c_up * up)
                    + (c_hi * hi + c_lo * lo)
                    + (c_ah * xp[c] + c_be * xm[c])
                )
            d_im = di[t]
            res = [None] * 4
            for h in range(2):
                d_re = dr[h, t]
                re, im = h, 2 + h
                res[re] = rhs_ref[0, h, t] - (
                    d_re * x[re] - d_im * x[im] - (nb[re] - LOSS_FACTOR * nb[im])
                )
                res[im] = rhs_ref[1, h, t] - (
                    d_re * x[im] + d_im * x[re] - (nb[im] + LOSS_FACTOR * nb[re])
                )
            return res

        def step(t, xm, x, xp, state):
            res = stencil(t, xm, x, xp)
            if final:
                for c in range(4):
                    sol_ref[c // 2, c % 2, t] = x[c]
                    res_ref[c // 2, c % 2, t] = res[c]
                return state
            y = [None] * 4
            for h in range(2):
                a, b = smooth(t, res[h], res[2 + h], h)
                y[h], y[2 + h] = x[h] + a, x[2 + h] + b
            for c in range(4):
                sol_ref[c // 2, c % 2, t] = y[c]
            sums = tuple(state[c] + res[c] for c in range(4))
            return sums + put_halo(k + 1, t, y, state[4:])

        def body(t, carry):
            xm, x, state = carry[0:4], carry[4:8], carry[8:]
            xp = tuple(load(t + 1))
            return tuple(x) + xp + tuple(step(t, xm, x, xp, state))

        state = () if final else (zero,) * 12
        carry = lax.fori_loop(0, ct - 1, body, tuple(before) + tuple(start) + state)
        state = step(ct - 1, carry[0:4], carry[4:8], beyond, carry[8:])
        if not final:
            restrict_and_send(k + 1, state[0:4])
            send_halo(k + 1, state[4:])
            mix_and_send(k + 1)

    on_faces(lambda d: stiff_copy(d).wait_send())
    for k in range(ITERS):
        on_faces(lambda d: halo_copy(k, d).wait_send())
        for d in range(1, nax):
            gather_one(k, d).wait_send()
        for d in range(1, nrad):
            gather_two(k, d).wait_send()


def local(rhs, mat_ids, stiff_table, dens_table, mass_shift, harmonic, radial_factor, axial_factor):
    nrad = lax.axis_size("radial")
    nax = lax.axis_size("axial")
    ct, rows, lanes = mat_ids.shape
    vmem = pl.BlockSpec(memory_space=pltpu.VMEM)
    smem = pl.BlockSpec(memory_space=pltpu.SMEM)
    f32 = jnp.float32
    field = (ct, rows, lanes)
    cdev = 4 * (rows // AR)
    dma = pltpu.SemaphoreType.DMA
    return pl.pallas_call(
        functools.partial(kernel, nrad, nax),
        out_shape=(jax.ShapeDtypeStruct(rhs.shape, f32), jax.ShapeDtypeStruct(rhs.shape, f32)),
        in_specs=[vmem, vmem, smem, smem, smem, smem, vmem, vmem],
        out_specs=(vmem, vmem),
        scratch_shapes=[
            pltpu.VMEM((ct + 2, rows, lanes), f32),
            pltpu.VMEM(field, f32),
            pltpu.VMEM(field, f32),
            pltpu.VMEM(field, f32),
            pltpu.VMEM(field, f32),
            pltpu.VMEM((ct + 1, rows, lanes), f32),
            pltpu.VMEM((2,) + field, f32),
            pltpu.VMEM(field, f32),
            pltpu.VMEM((2,) + field, f32),
            pltpu.VMEM((2, ct, lanes), f32),
            pltpu.VMEM((2, ct, lanes), f32),
            pltpu.VMEM((2, rows, lanes), f32),
            pltpu.VMEM((2, rows, lanes), f32),
            pltpu.VMEM((ITERS, 2, 4, ct, lanes), f32),
            pltpu.VMEM((ITERS, 2, 4, ct, lanes), f32),
            pltpu.VMEM((ITERS, 2, 4, rows, lanes), f32),
            pltpu.VMEM((ITERS, 2, 4, rows, lanes), f32),
            pltpu.VMEM((ITERS, rows, lanes), f32),
            pltpu.VMEM((ITERS, nax, rows, lanes), f32),
            pltpu.VMEM((ITERS, nrad, rows, 2 * lanes), f32),
            pltpu.VMEM((2, 3 * lanes, lanes), f32),
            pltpu.VMEM((8 * rows, nrad * cdev), f32),
            dma((4,)),
            dma((4,)),
            dma((ITERS, 4)),
            dma((ITERS, 4)),
            dma((ITERS, nax)),
            dma((ITERS, nax)),
            dma((ITERS, nrad)),
            dma((ITERS, nrad)),
        ],
        compiler_params=pltpu.CompilerParams(
            collective_id=0, has_side_effects=True, vmem_limit_bytes=40 * 1024 * 1024
        ),
    )(rhs, mat_ids, stiff_table, dens_table, mass_shift, harmonic, radial_factor, axial_factor)


def solution(mesh):
    return jax.shard_map(
        local,
        mesh=mesh,
        in_specs=(
            P(None, None, None, "radial", "axial"),
            P(None, "radial", "axial"),
            P(),
            P(),
            P(),
            P(),
            P(),
            P(),
        ),
        out_specs=(P(None, None, None, "radial", "axial"), P(None, None, None, "radial", "axial")),
        check_vma=False,
    )
```

time: 397 us -> 105 us (0.26)
  the two profiles are of different devices: /device:TPU:12 before, /device:TPU:0 now
where the time goes in v1:
time: 105 us
  Pallas kernels  95.5 us (91%)
  local copies, waits for them, and re-layouts  8.96 us (9%)
    pallas_call x1, Pallas kernels, local(): pl.pallas_call(functools.partial(kernel, nrad, nax), out_shape=(jax.Shape...  95.5 us
    unnamed x18, local copies, waits for them, and re-layouts  8.96 us

profile of v1, /device:TPU:0, one launch (start us, length us, event | category | flops | bytes accessed | tf_op | source)
XLA Modules:
  0.0 105.1 jit_solution(16574656392662771768)
XLA Ops:
  0.6 0.0 copy-start
  0.6 1.4 %copy-done = f32[2,2,96,8,128]{4,3,2,1,0:T(8,128)S(1)} copy-done((f32[2,2,96,8,128]{4,3,2,1,0:T(8,128)S(1)}, f32[2,2,96,8,128]{4,3,2,1,0:T(8,128)}, u32[]{:S(2)}) %copy-start) | copy-done | bytes 1572888
  2.0 0.0 copy-start.1
  2.0 1.0 copy-done.1
  3.0 0.0 copy-start.2
  3.0 0.9 copy-done.2
  3.9 0.0 copy-start.3
  3.9 0.8 copy-done.3
  4.7 0.0 copy-start.4
  4.7 0.7 copy-done.4
  5.4 0.0 copy-start.5
  5.4 0.7 copy-done.5
  6.0 0.0 copy-start.6
  6.0 0.7 copy-done.6
  6.7 0.0 copy-start.7
  6.7 0.7 copy-done.7
  7.3 95.5 %shard_map.95 = (f32[2,2,96,8,128]{4,3,2,1,0:T(8,128)S(1)}, f32[2,2,96,8,128]{4,3,2,1,0:T(8,128)S(1)}) custom-call(f32[2,2,96,8,128]{4,3,2,1,0:T(8,128)S(1)} %copy-done, s32[96,8,128]{2,1,0:T(8,128)S(1)} %copy-done.1, f32[4]{0:T(128)S(1)} %copy-done.4, f32[4]{0:T(128)S(1)} %copy-done.5, f32[2]{0:T(128)S(1)} %copy-done.6, s32[2]{0:T(128)S(1)} %copy-done.7, ...), custom_call_target="tpu_custom_call" | custom-call | tf_op jit(solution)/shard_map/pallas_call | solution.py:501
  102.8 1.1 %copy.12 = f32[2,2,96,8,128]{4,3,2,1,0:T(8,128)} copy(f32[2,2,96,8,128]{4,3,2,1,0:T(8,128)S(1)} %get-tuple-element.4) | data formatting | bytes 3145728
  104.0 1.1 %copy.13 = f32[2,2,96,8,128]{4,3,2,1,0:T(8,128)} copy(f32[2,2,96,8,128]{4,3,2,1,0:T(8,128)S(1)} %get-tuple-element.5) | data formatting | bytes 3145728
Async XLA Ops:
  0.6 1.4 %copy-start = (f32[2,2,96,8,128]{4,3,2,1,0:T(8,128)S(1)}, f32[2,2,96,8,128]{4,3,2,1,0:T(8,128)}, u32[]{:S(2)}) copy-start(f32[2,2,96,8,128]{4,3,2,1,0:T(8,128)} %rhs_ref.1) | copy-start | bytes 4718596
  2.0 1.0 copy-start.1
  3.0 0.9 copy-start.2
  3.9 0.8 copy-start.3
  4.7 0.7 copy-start.4
  5.4 0.7 copy-start.5
  6.0 0.7 copy-start.6
  6.7 0.7 copy-start.7

commit v2 on v1

--- a/solution.py
+++ b/solution.py
@@ -15,11 +15,22 @@
 RELAXATION = 0.6
 MESH = pl.DeviceIdType.MESH
 HIGHEST = lax.Precision.HIGHEST
+CHUNK = 8
 
 
 def kernel(
     nrad,
     nax,
+    rhs_hbm,
+    ids_hbm,
+    stiff_hbm,
+    dens_hbm,
+    mass_hbm,
+    harm_hbm,
+    radial_hbm,
+    axial_hbm,
+    sol_ref,
+    res_ref,
     rhs_ref,
     ids_ref,
     stiff_ref,
@@ -28,8 +39,7 @@
     harm_ref,
     radial_ref,
     axial_ref,
-    sol_ref,
-    res_ref,
+    in_sem,
     stiff,
     wr_up,
     wr_dn,
@@ -47,6 +57,7 @@
     row_r,
     col_s,
     col_r,
+    col_m,
     one_s,
     one_r,
     two_r,
@@ -61,6 +72,23 @@
     g2_send,
     g2_recv,
 ):
+    loads = [
+        pltpu.make_async_copy(src, dst, in_sem.at[n])
+        for n, (src, dst) in enumerate(
+            (
+                (stiff_hbm, stiff_ref),
+                (ids_hbm, ids_ref),
+                (rhs_hbm, rhs_ref),
+                (dens_hbm, dens_ref),
+                (mass_hbm, mass_ref),
+                (harm_hbm, harm_ref),
+                (radial_hbm, radial_ref),
+                (axial_hbm, axial_ref),
+            )
+        )
+    ]
+    for load_in in loads:
+        load_in.start()
     ct = rhs_ref.shape[2]
     rows, lanes = rhs_ref.shape[3:]
     gr = radial_ref.shape[2]
@@ -107,16 +135,18 @@
             value = jnp.where(ids == entry, table[entry], value)
         return value
 
-    def pack(value, t, first, last):
-        first = jnp.where(lane == t, pltpu.roll(value, t, 1), first)
-        last = jnp.where(lane == t, pltpu.roll(value, t + 1, 1), last)
-        return first, last
+    cap = lanes // 2
+    pair = lane // 2
+
+    def pack(value, t, packed):
+        at = lax.rem(t, cap)
+        return jnp.where(pair == at, pltpu.roll(value, 2 * at + 1, 1), packed)
 
     def stiff_copy(d):
         if d < 2:
             src, dst = srow_s.at[d], srow_r.at[1 - d]
         else:
-            src, dst = scol_s.at[d - 2], scol_r.at[3 - d]
+            src, dst = scol_s, scol_r.at[3 - d]
         return pltpu.make_async_remote_copy(
             src_ref=src,
             dst_ref=dst,
@@ -130,7 +160,7 @@
         if d < 2:
             src, dst = row_s.at[k, d], row_r.at[k, 1 - d]
         else:
-            src, dst = col_s.at[k, d - 2], col_r.at[k, 3 - d]
+            src, dst = col_s.at[k], col_r.at[k, 3 - d]
         return pltpu.make_async_remote_copy(
             src_ref=src,
             dst_ref=dst,
@@ -167,25 +197,25 @@
             def _():
                 act(d)
 
-    def first_pass(t, carry):
-        first, last, s0, s1, s2, s3 = carry
-        value = lookup(ids_ref[t], stiff_ref)
-        stiff[t + 1] = value
-        srow_s[0, pl.ds(t, 1), :] = value[0:1]
-        srow_s[1, pl.ds(t, 1), :] = value[rows - 1 : rows]
-        first, last = pack(value, t, first, last)
-        return (
-            first,
-            last,
-            s0 + rhs_ref[0, 0, t],
-            s1 + rhs_ref[0, 1, t],
-            s2 + rhs_ref[1, 0, t],
-            s3 + rhs_ref[1, 1, t],
-        )
-
-    first, last, *sums = lax.fori_loop(0, ct, first_pass, (zero,) * 6)
-    scol_s[0] = first
-    scol_s[1] = last
+    scol_s[...] = jnp.zeros(scol_s.shape, jnp.float32)
+    col_s[...] = jnp.zeros(col_s.shape, jnp.float32)
+    loads[0].wait()
+    loads[1].wait()
+
+    @pl.loop(0, ct // CHUNK)
+    def _(chunk):
+        begin = chunk * CHUNK
+        tile = begin // cap
+        packed = scol_s[tile]
+        for u in range(CHUNK):
+            t = begin + u
+            value = lookup(ids_ref[t], stiff_ref)
+            stiff[t + 1] = value
+            srow_s[0, pl.ds(t, 1), :] = value[0:1]
+            srow_s[1, pl.ds(t, 1), :] = value[rows - 1 : rows]
+            packed = pack(value, t, packed)
+        scol_s[tile] = packed
+
     stiff[0] = stiff[ct]
     stiff[ct + 1] = stiff[1]
 
@@ -209,7 +239,18 @@
         for d in range(1, nax):
             gather_one(k, d).start()
 
-    restrict_and_send(0, sums)
+    loads[2].wait()
+
+    def sum_pass(chunk, sums):
+        sums = list(sums)
+        for u in range(CHUNK):
+            for c in range(4):
+                sums[c] = sums[c] + rhs_ref[c // 2, c % 2, chunk * CHUNK + u]
+        return tuple(sums)
+
+    restrict_and_send(0, lax.fori_loop(0, ct // CHUNK, sum_pass, (zero,) * 4))
+    for load_in in loads[3:]:
+        load_in.wait()
 
     ax_row = lax.broadcasted_iota(jnp.int32, (lanes, ga), 0)
     ax_col = lax.broadcasted_iota(jnp.int32, (lanes, ga), 1)
@@ -317,34 +358,36 @@
 
     mass = [mass_ref[0], mass_ref[1]]
 
-    def around(value, up, dn, lo, hi, t):
+    odd_lane = lane % 2 == 1
+
+    def around(value, up, dn, beside, t):
+        edge = pltpu.roll(beside, lanes - 1 - 2 * lax.rem(t, cap), 1)
         return (
             jnp.where(row == 0, up, pltpu.roll(value, 1, 0)),
             jnp.where(row == rows - 1, dn, pltpu.roll(value, rows - 1, 0)),
-            jnp.where(lane == 0, pltpu.roll(lo, lax.rem(lanes - t, lanes), 1), pltpu.roll(value, 1, 1)),
-            jnp.where(lane == lanes - 1, pltpu.roll(hi, lanes - 1 - t, 1), pltpu.roll(value, lanes - 1, 1)),
-        )
-
-    def put_halo(k, t, y, packs):
-        out = []
+            pltpu.roll(jnp.where(lane == lanes - 1, edge, value), 1, 1),
+            pltpu.roll(jnp.where(lane == 0, edge, value), lanes - 1, 1),
+        )
+
+    def put_rows(k, t, y):
         for c in range(4):
             row_s[k, 0, c, pl.ds(t, 1), :] = y[c][0:1]
             row_s[k, 1, c, pl.ds(t, 1), :] = y[c][rows - 1 : rows]
-            out.extend(pack(y[c], t, packs[2 * c], packs[2 * c + 1]))
-        return tuple(out)
 
     def smooth(t, rr, ri, h):
         d_re, d_im, scale = dr[h, t], di[t], sc[h, t]
         return (d_re * rr + d_im * ri) * scale, (d_re * ri - d_im * rr) * scale
 
-    def setup_pass(t, packs):
+    for n in range(scol_s.shape[0]):
+        col_m[0, n] = jnp.where(odd_lane, scol_r[1, n], scol_r[0, n])
+
+    def setup_step(t, packs, beside):
         value = stiff[t + 1]
         up, dn, lo, hi = around(
             value,
             srow_r[0, pl.ds(t, 1), :],
             srow_r[1, pl.ds(t, 1), :],
-            scol_r[0],
-            scol_r[1],
+            beside,
             t,
         )
         c_up, c_dn = 0.5 * (value + up), 0.5 * (value + dn)
@@ -371,15 +414,21 @@
             y[2 + h] = (d_re * ri - d_im * rr) * scale
             sol_ref[0, h, t] = y[h]
             sol_ref[1, h, t] = y[2 + h]
-        return put_halo(0, t, y, packs)
-
-    def send_halo(k, packs):
+        put_rows(0, t, y)
+        return [pack(y[c], t, packs[c]) for c in range(4)]
+
+    @pl.loop(0, ct // CHUNK)
+    def _(chunk):
+        begin = chunk * CHUNK
+        tile = begin // cap
+        beside = col_m[0, tile]
+        packs = [col_s[0, c, tile] for c in range(4)]
+        for u in range(CHUNK):
+            packs = setup_step(begin + u, packs, beside)
         for c in range(4):
-            col_s[k, 0, c] = packs[2 * c]
-            col_s[k, 1, c] = packs[2 * c + 1]
-        on_faces(lambda d: halo_copy(k, d).start())
-
-    send_halo(0, lax.fori_loop(0, ct, setup_pass, (zero,) * 8))
+            col_s[0, c, tile] = packs[c]
+
+    on_faces(lambda d: halo_copy(0, d).start())
 
     cosines, sines = [], []
     for h in range(2):
@@ -394,18 +443,16 @@
         coarse = finish_coarse(k)
         corr = [coarse[c * per : c * per + rows, 0:lanes] for c in range(4)]
         on_faces(lambda d: halo_copy(k, d ^ 1).wait_recv())
-        cols = []
         for c in range(4):
-            for s in range(2):
-                at = c * per + rows + s
-                row_r[k, s, c] = row_r[k, s, c] + coarse[at : at + 1, 0:lanes]
-                cols.append(
-                    col_r[k, s, c]
-                    + coarse[c * per : c * per + rows, lanes + s : lanes + s + 1]
+            add = []
+            for side in range(2):
+                at = c * per + rows + side
+                row_r[k, side, c] = row_r[k, side, c] + coarse[at : at + 1, 0:lanes]
+                add.append(coarse[c * per : c * per + rows, lanes + side : lanes + side + 1])
+            for n in range(col_m.shape[1]):
+                col_m[c, n] = jnp.where(
+                    odd_lane, col_r[k, 1, c, n] + add[1], col_r[k, 0, c, n] + add[0]
                 )
-        for c in range(4):
-            col_r[k, 0, c] = cols[2 * c]
-            col_r[k, 1, c] = cols[2 * c + 1]
 
         def load(t):
             return [sol_ref[c // 2, c % 2, t] + corr[c] for c in range(4)]
@@ -419,7 +466,7 @@
         beyond = turn(start, 1.0)
         before = turn(load(ct - 1), -1.0)
 
-        def stencil(t, xm, x, xp):
+        def stencil(t, xm, x, xp, beside):
             c_up, c_dn, c_lo, c_hi = wr_up[t], wr_dn[t], wa_lo[t], wa_hi[t]
             c_be, c_ah = wt[t], wt[t + 1]
             nb = []
@@ -428,8 +475,7 @@
                     x[c],
                     row_r[k, 0, c, pl.ds(t, 1), :],
                     row_r[k, 1, c, pl.ds(t, 1), :],
-                    col_r[k, 0, c],
-                    col_r[k, 1, c],
+                    beside[c],
                     t,
                 )
                 nb.append(
@@ -450,33 +496,47 @@
                 )
             return res
 
-        def step(t, xm, x, xp, state):
-            res = stencil(t, xm, x, xp)
-            if final:
+        def chunk_pass(chunk, carry):
+            xm, x, sums = list(carry[0:4]), list(carry[4:8]), list(carry[8:])
+            begin = chunk * CHUNK
+            tile = begin // cap
+            beside = [col_m[c, tile] for c in range(4)]
+            if not final:
+                packs = [col_s[k + 1, c, tile] for c in range(4)]
+            for u in range(CHUNK):
+                t = begin + u
+                if u < CHUNK - 1:
+                    xp = load(t + 1)
+                else:
+                    ended = t == ct - 1
+                    xp = load(jnp.minimum(t + 1, ct - 1))
+                    xp = [jnp.where(ended, beyond[c], xp[c]) for c in range(4)]
+                res = stencil(t, xm, x, xp, beside)
+                if final:
+                    for c in range(4):
+                        sol_ref[c // 2, c % 2, t] = x[c]
+                        res_ref[c // 2, c % 2, t] = res[c]
+                else:
+                    y = [None] * 4
+                    for h in range(2):
+                        a, b = smooth(t, res[h], res[2 + h], h)
+                        y[h], y[2 + h] = x[h] + a, x[2 + h] + b
+                    for c in range(4):
+                        sol_ref[c // 2, c % 2, t] = y[c]
+                        sums[c] = sums[c] + res[c]
+                        packs[c] = pack(y[c], t, packs[c])
+                    put_rows(k + 1, t, y)
+                xm, x = x, xp
+            if not final:
                 for c in range(4):
-                    sol_ref[c // 2, c % 2, t] = x[c]
-                    res_ref[c // 2, c % 2, t] = res[c]
-                return state
-            y = [None] * 4
-            for h in range(2):
-                a, b = smooth(t, res[h], res[2 + h], h)
-                y[h], y[2 + h] = x[h] + a, x[2 + h] + b
-            for c in range(4):
-                sol_ref[c // 2, c % 2, t] = y[c]
-            sums = tuple(state[c] + res[c] for c in range(4))
-            return sums + put_halo(k + 1, t, y, state[4:])
-
-        def body(t, carry):
-            xm, x, state = carry[0:4], carry[4:8], carry[8:]
-            xp = tuple(load(t + 1))
-            return tuple(x) + xp + tuple(step(t, xm, x, xp, state))
-
-        state = () if final else (zero,) * 12
-        carry = lax.fori_loop(0, ct - 1, body, tuple(before) + tuple(start) + state)
-        state = step(ct - 1, carry[0:4], carry[4:8], beyond, carry[8:])
+                    col_s[k + 1, c, tile] = packs[c]
+            return tuple(xm) + tuple(x) + tuple(sums)
+
+        state = () if final else (zero,) * 4
+        carry = lax.fori_loop(0, ct // CHUNK, chunk_pass, tuple(before) + tuple(start) + state)
         if not final:
-            restrict_and_send(k + 1, state[0:4])
-            send_halo(k + 1, state[4:])
+            restrict_and_send(k + 1, carry[8:])
+            on_faces(lambda d: halo_copy(k + 1, d).start())
             mix_and_send(k + 1)
 
     on_faces(lambda d: stiff_copy(d).wait_send())
@@ -493,7 +553,8 @@
     nax = lax.axis_size("axial")
     ct, rows, lanes = mat_ids.shape
     vmem = pl.BlockSpec(memory_space=pltpu.VMEM)
-    smem = pl.BlockSpec(memory_space=pltpu.SMEM)
+    hbm = pl.BlockSpec(memory_space=pltpu.HBM)
+    tiles = -(-2 * ct // lanes)
     f32 = jnp.float32
     field = (ct, rows, lanes)
     cdev = 4 * (rows // AR)
@@ -501,9 +562,18 @@
     return pl.pallas_call(
         functools.partial(kernel, nrad, nax),
         out_shape=(jax.ShapeDtypeStruct(rhs.shape, f32), jax.ShapeDtypeStruct(rhs.shape, f32)),
-        in_specs=[vmem, vmem, smem, smem, smem, smem, vmem, vmem],
+        in_specs=[hbm] * 8,
         out_specs=(vmem, vmem),
         scratch_shapes=[
+            pltpu.VMEM(rhs.shape, f32),
+            pltpu.VMEM(field, jnp.int32),
+            pltpu.SMEM(stiff_table.shape, f32),
+            pltpu.SMEM(dens_table.shape, f32),
+            pltpu.SMEM(mass_shift.shape, f32),
+            pltpu.SMEM(harmonic.shape, jnp.int32),
+            pltpu.VMEM(radial_factor.shape, f32),
+            pltpu.VMEM(axial_factor.shape, f32),
+            dma((8,)),
             pltpu.VMEM((ct + 2, rows, lanes), f32),
             pltpu.VMEM(field, f32),
             pltpu.VMEM(field, f32),
@@ -515,12 +585,13 @@
             pltpu.VMEM((2,) + field, f32),
             pltpu.VMEM((2, ct, lanes), f32),
             pltpu.VMEM((2, ct, lanes), f32),
-            pltpu.VMEM((2, rows, lanes), f32),
-            pltpu.VMEM((2, rows, lanes), f32),
+            pltpu.VMEM((tiles, rows, lanes), f32),
+            pltpu.VMEM((2, tiles, rows, lanes), f32),
             pltpu.VMEM((ITERS, 2, 4, ct, lanes), f32),
             pltpu.VMEM((ITERS, 2, 4, ct, lanes), f32),
-            pltpu.VMEM((ITERS, 2, 4, rows, lanes), f32),
-            pltpu.VMEM((ITERS, 2, 4, rows, lanes), f32),
+            pltpu.VMEM((ITERS, 4, tiles, rows, lanes), f32),
+            pltpu.VMEM((ITERS, 2, 4, tiles, rows, lanes), f32),
+            pltpu.VMEM((4, tiles, rows, lanes), f32),
             pltpu.VMEM((ITERS, rows, lanes), f32),
             pltpu.VMEM((ITERS, nax, rows, lanes), f32),
             pltpu.VMEM((ITERS, nrad, rows, 2 * lanes), f32),
@@ -536,7 +607,7 @@
             dma((ITERS, nrad)),
         ],
         compiler_params=pltpu.CompilerParams(
-            collective_id=0, has_side_effects=True, vmem_limit_bytes=40 * 1024 * 1024
+            collective_id=0, has_side_effects=True, vmem_limit_bytes=58 * 1024 * 1024
         ),
     )(rhs, mat_ids, stiff_table, dens_table, mass_shift, harmonic, radial_factor, axial_factor)
 

time: 105 us -> 51.1 us (0.49)
  Pallas kernels: 95.5 us -> 46.4 us
  local copies, waits for them, and re-layouts: 8.96 us -> 3.92 us
    pallas_call x1, Pallas kernels: 95.5 us -> 46.4 us  [local(): pl.pallas_call(functools.partial(kernel, nrad, nax), out_shape=(jax.Shape...]
    unnamed x18 -> x4, local copies, waits for them, and re-layouts: 8.96 us -> 3.92 us
where the time goes in v2:
time: 51.1 us; the launch traced here: 51 us
  Pallas kernels  46.4 us (91%)
  local copies, waits for them, and re-layouts  3.92 us (8%)
  between operations  0.65 us (1%)
    pallas_call x1, Pallas kernels, local(): pl.pallas_call(functools.partial(kernel, nrad, nax), out_shape=(jax.Shape...  46.4 us
    unnamed x4, local copies, waits for them, and re-layouts  3.92 us

profile of v2, /device:TPU:0, one launch (start us, length us, event | category | flops | bytes accessed | tf_op | source)
XLA Modules:
  0.0 51.0 jit_solution(7039268259615032910)
XLA Ops:
  0.6 46.4 %shard_map.95 = (f32[2,2,96,8,128]{4,3,2,1,0:T(8,128)}, f32[2,2,96,8,128]{4,3,2,1,0:T(8,128)}) custom-call(f32[2,2,96,8,128]{4,3,2,1,0:T(8,128)} %rhs_hbm.1, s32[96,8,128]{2,1,0:T(8,128)} %ids_hbm.1, f32[4]{0:T(128)} %stiff_hbm.1, f32[4]{0:T(128)} %dens_hbm.1, f32[2]{0:T(128)} %mass_hbm.1, s32[2]{0:T(128)} %harm_hbm.1, f32[2,2,16,16]{3,2,1,0:T(8,128)} %radial_hbm.1, ...), custom_call_target="tpu_custom_call" | custom-call | tf_op jit(solution)/shard_map/pallas_call | solution.py:562
  47.0 0.0 copy-start
  47.0 2.8 %copy.12 = f32[2,2,96,8,128]{4,3,2,1,0:T(8,128)} copy(f32[2,2,96,8,128]{4,3,2,1,0:T(8,128)} %get-tuple-element.4) | data formatting | bytes 3145728
  49.8 0.0 copy-done
  49.8 1.1 %copy.13 = f32[2,2,96,8,128]{4,3,2,1,0:T(8,128)} copy(f32[2,2,96,8,128]{4,3,2,1,0:T(8,128)S(1)} %copy-done) | data formatting | bytes 3145728
Async XLA Ops:
  47.0 2.8 %copy-start = (f32[2,2,96,8,128]{4,3,2,1,0:T(8,128)S(1)}, f32[2,2,96,8,128]{4,3,2,1,0:T(8,128)}, u32[]{:S(2)}) copy-start(f32[2,2,96,8,128]{4,3,2,1,0:T(8,128)} %get-tuple-element.5) | copy-start | bytes 4718596

commit v3 on v2

--- a/solution.py
+++ b/solution.py
@@ -156,16 +156,19 @@
             device_id_type=MESH,
         )
 
-    def halo_copy(k, d):
+    middle = 3 * (ct // CHUNK) // 4
+
+    def halo_copy(k, d, late=1):
         if d < 2:
-            src, dst = row_s.at[k, d], row_r.at[k, 1 - d]
+            part = pl.ds(middle * CHUNK, ct - middle * CHUNK) if late else pl.ds(0, middle * CHUNK)
+            src, dst = row_s.at[k, d, :, part], row_r.at[k, 1 - d, :, part]
         else:
             src, dst = col_s.at[k], col_r.at[k, 3 - d]
         return pltpu.make_async_remote_copy(
             src_ref=src,
             dst_ref=dst,
-            send_sem=ha_send.at[k, d],
-            recv_sem=ha_recv.at[k, d ^ 1],
+            send_sem=ha_send.at[k, late, d],
+            recv_sem=ha_recv.at[k, late, d ^ 1],
             device_id=targets[d],
             device_id_type=MESH,
         )
@@ -190,8 +193,8 @@
             device_id_type=MESH,
         )
 
-    def on_faces(act):
-        for d in range(4):
+    def on_faces(act, faces=4):
+        for d in range(faces):
 
             @pl.when(conds[d])
             def _():
@@ -417,8 +420,7 @@
         put_rows(0, t, y)
         return [pack(y[c], t, packs[c]) for c in range(4)]
 
-    @pl.loop(0, ct // CHUNK)
-    def _(chunk):
+    def setup_chunk(chunk, nothing):
         begin = chunk * CHUNK
         tile = begin // cap
         beside = col_m[0, tile]
@@ -427,7 +429,11 @@
             packs = setup_step(begin + u, packs, beside)
         for c in range(4):
             col_s[0, c, tile] = packs[c]
-
+        return nothing
+
+    lax.fori_loop(0, middle, setup_chunk, 0)
+    on_faces(lambda d: halo_copy(0, d, 0).start(), 2)
+    lax.fori_loop(middle, ct // CHUNK, setup_chunk, 0)
     on_faces(lambda d: halo_copy(0, d).start())
 
     cosines, sines = [], []
@@ -442,6 +448,7 @@
         final = k == ITERS - 1
         coarse = finish_coarse(k)
         corr = [coarse[c * per : c * per + rows, 0:lanes] for c in range(4)]
+        on_faces(lambda d: halo_copy(k, d ^ 1, 0).wait_recv(), 2)
         on_faces(lambda d: halo_copy(k, d ^ 1).wait_recv())
         for c in range(4):
             add = []
@@ -533,7 +540,13 @@
             return tuple(xm) + tuple(x) + tuple(sums)
 
         state = () if final else (zero,) * 4
-        carry = lax.fori_loop(0, ct // CHUNK, chunk_pass, tuple(before) + tuple(start) + state)
+        carry = tuple(before) + tuple(start) + state
+        if final:
+            lax.fori_loop(0, ct // CHUNK, chunk_pass, carry)
+        else:
+            carry = lax.fori_loop(0, middle, chunk_pass, carry)
+            on_faces(lambda d: halo_copy(k + 1, d, 0).start(), 2)
+            carry = lax.fori_loop(middle, ct // CHUNK, chunk_pass, carry)
         if not final:
             restrict_and_send(k + 1, carry[8:])
             on_faces(lambda d: halo_copy(k + 1, d).start())
@@ -541,6 +554,7 @@
 
     on_faces(lambda d: stiff_copy(d).wait_send())
     for k in range(ITERS):
+        on_faces(lambda d: halo_copy(k, d, 0).wait_send(), 2)
         on_faces(lambda d: halo_copy(k, d).wait_send())
         for d in range(1, nax):
             gather_one(k, d).wait_send()
@@ -599,8 +613,8 @@
             pltpu.VMEM((8 * rows, nrad * cdev), f32),
             dma((4,)),
             dma((4,)),
-            dma((ITERS, 4)),
-            dma((ITERS, 4)),
+            dma((ITERS, 2, 4)),
+            dma((ITERS, 2, 4)),
             dma((ITERS, nax)),
             dma((ITERS, nax)),
             dma((ITERS, nrad)),

time: 51.1 us -> 50.1 us (0.980)
  Pallas kernels: 46.4 us -> 45.3 us
    pallas_call x1, Pallas kernels: 46.4 us -> 45.3 us  [local(): pl.pallas_call(functools.partial(kernel, nrad, nax), out_shape=(jax.Shape...]
where the time goes in v3:
time: 50.1 us; the launch traced here: 49.9 us
  Pallas kernels  45.3 us (90%)
  local copies, waits for them, and re-layouts  3.92 us (8%)
  between operations  0.65 us (1%)
    pallas_call x1, Pallas kernels, local(): pl.pallas_call(functools.partial(kernel, nrad, nax), out_shape=(jax.Shape...  45.3 us
    unnamed x4, local copies, waits for them, and re-layouts  3.92 us

profile of v3, /device:TPU:0, one launch (start us, length us, event | category | flops | bytes accessed | tf_op | source)
XLA Modules:
  0.0 49.9 jit_solution(12599899695085496818)
XLA Ops:
  0.6 45.3 %shard_map.95 = (f32[2,2,96,8,128]{4,3,2,1,0:T(8,128)}, f32[2,2,96,8,128]{4,3,2,1,0:T(8,128)}) custom-call(f32[2,2,96,8,128]{4,3,2,1,0:T(8,128)} %rhs_hbm.1, s32[96,8,128]{2,1,0:T(8,128)} %ids_hbm.1, f32[4]{0:T(128)} %stiff_hbm.1, f32[4]{0:T(128)} %dens_hbm.1, f32[2]{0:T(128)} %mass_hbm.1, s32[2]{0:T(128)} %harm_hbm.1, f32[2,2,16,16]{3,2,1,0:T(8,128)} %radial_hbm.1, ...), custom_call_target="tpu_custom_call" | custom-call | tf_op jit(solution)/shard_map/pallas_call | solution.py:576
  46.0 0.0 copy-start
  46.0 2.8 %copy.12 = f32[2,2,96,8,128]{4,3,2,1,0:T(8,128)} copy(f32[2,2,96,8,128]{4,3,2,1,0:T(8,128)} %get-tuple-element.4) | data formatting | bytes 3145728
  48.7 0.0 copy-done
  48.8 1.1 %copy.13 = f32[2,2,96,8,128]{4,3,2,1,0:T(8,128)} copy(f32[2,2,96,8,128]{4,3,2,1,0:T(8,128)S(1)} %copy-done) | data formatting | bytes 3145728
Async XLA Ops:
  46.0 2.8 %copy-start = (f32[2,2,96,8,128]{4,3,2,1,0:T(8,128)S(1)}, f32[2,2,96,8,128]{4,3,2,1,0:T(8,128)}, u32[]{:S(2)}) copy-start(f32[2,2,96,8,128]{4,3,2,1,0:T(8,128)} %get-tuple-element.5) | copy-start | bytes 4718596

commit v4 on v3

--- a/solution.py
+++ b/solution.py
@@ -156,7 +156,7 @@
             device_id_type=MESH,
         )
 
-    middle = 3 * (ct // CHUNK) // 4
+    middle = 5 * (ct // CHUNK) // 6
 
     def halo_copy(k, d, late=1):
         if d < 2:
@@ -246,12 +246,12 @@
 
     def sum_pass(chunk, sums):
         sums = list(sums)
-        for u in range(CHUNK):
+        for u in range(2 * CHUNK):
             for c in range(4):
-                sums[c] = sums[c] + rhs_ref[c // 2, c % 2, chunk * CHUNK + u]
+                sums[c] = sums[c] + rhs_ref[c // 2, c % 2, chunk * 2 * CHUNK + u]
         return tuple(sums)
 
-    restrict_and_send(0, lax.fori_loop(0, ct // CHUNK, sum_pass, (zero,) * 4))
+    restrict_and_send(0, lax.fori_loop(0, ct // (2 * CHUNK), sum_pass, (zero,) * 4))
     for load_in in loads[3:]:
         load_in.wait()
 

time: 50.1 us -> 50.2 us (level)
  no operation moved by 1% of the time
where the time goes in v4:
time: 50.2 us; the launch traced here: 50.1 us
  Pallas kernels  45.5 us (91%)
  local copies, waits for them, and re-layouts  3.92 us (8%)
  between operations  0.65 us (1%)
    pallas_call x1, Pallas kernels, local(): pl.pallas_call(functools.partial(kernel, nrad, nax), out_shape=(jax.Shape...  45.5 us
    unnamed x4, local copies, waits for them, and re-layouts  3.92 us

profile of v4, /device:TPU:0, one launch (start us, length us, event | category | flops | bytes accessed | tf_op | source)
XLA Modules:
  0.0 50.1 jit_solution(18249140081770912263)
XLA Ops:
  0.6 45.5 %shard_map.95 = (f32[2,2,96,8,128]{4,3,2,1,0:T(8,128)}, f32[2,2,96,8,128]{4,3,2,1,0:T(8,128)}) custom-call(f32[2,2,96,8,128]{4,3,2,1,0:T(8,128)} %rhs_hbm.1, s32[96,8,128]{2,1,0:T(8,128)} %ids_hbm.1, f32[4]{0:T(128)} %stiff_hbm.1, f32[4]{0:T(128)} %dens_hbm.1, f32[2]{0:T(128)} %mass_hbm.1, s32[2]{0:T(128)} %harm_hbm.1, f32[2,2,16,16]{3,2,1,0:T(8,128)} %radial_hbm.1, ...), custom_call_target="tpu_custom_call" | custom-call | tf_op jit(solution)/shard_map/pallas_call | solution.py:576
  46.2 0.0 copy-start
  46.2 2.8 %copy.12 = f32[2,2,96,8,128]{4,3,2,1,0:T(8,128)} copy(f32[2,2,96,8,128]{4,3,2,1,0:T(8,128)} %get-tuple-element.4) | data formatting | bytes 3145728
  48.9 0.0 copy-done
  48.9 1.1 %copy.13 = f32[2,2,96,8,128]{4,3,2,1,0:T(8,128)} copy(f32[2,2,96,8,128]{4,3,2,1,0:T(8,128)S(1)} %copy-done) | data formatting | bytes 3145728
Async XLA Ops:
  46.2 2.8 %copy-start = (f32[2,2,96,8,128]{4,3,2,1,0:T(8,128)S(1)}, f32[2,2,96,8,128]{4,3,2,1,0:T(8,128)}, u32[]{:S(2)}) copy-start(f32[2,2,96,8,128]{4,3,2,1,0:T(8,128)} %get-tuple-element.5) | copy-start | bytes 4718596
